TPU v7x, 256 devices: a whole 4x4x8 slice. The times are simulated.
256 devices in a mesh: gossip: 128 (over x_lo, y, z, core), dp: 2 (over x_hi).
Axes of the slice: x: 4 (x_hi: 2, x_lo: 2; x = x_hi * 2 + x_lo), y: 4, z: 8, core: 2. Of those that a mesh axis runs over, the one named last changes fastest.
Arguments:
- images: bfloat16 [256, 28, 28, 512], P(('gossip', 'dp')), may hold values from -6 to 6
- cotangent: bfloat16 [256, 28, 28, 512], P(('gossip', 'dp')), may hold values from -6 to 6
- w_first: float32 [128, 512, 128], P('gossip', 'dp'), may hold values from -6 to 6
- w_middle: float32 [128, 1152, 128], P('gossip', 'dp'), may hold values from -6 to 6
- w_last: float32 [128, 128, 512], P('gossip', None, 'dp'), may hold values from -6 to 6
- m_first: float32 [128, 512, 128], P('gossip', 'dp'), may hold values from -6 to 6
- m_middle: float32 [128, 1152, 128], P('gossip', 'dp'), may hold values from -6 to 6
- m_last: float32 [128, 128, 512], P('gossip', None, 'dp'), may hold values from -6 to 6
Outputs:
- new_first: float32 [128, 512, 128], P('gossip', 'dp')
- new_middle: float32 [128, 1152, 128], P('gossip', 'dp')
- new_last: float32 [128, 128, 512], P('gossip', None, 'dp')
- mom_first: float32 [128, 512, 128], P('gossip', 'dp')
- mom_middle: float32 [128, 1152, 128], P('gossip', 'dp')
- mom_last: float32 [128, 128, 512], P('gossip', None, 'dp')
All inputs are finite; a program needn't handle non-finite values.
Results may differ from a plain program's by a relative error of at most 0.0065.
Values may be sent and summed in bfloat16 or wider, within the bound.
A program may use at most 64 MiB of HBM per device.

v0:
```python
import jax
import jax.numpy as jnp
from jax import lax
from jax.sharding import PartitionSpec as P

CIN = 512
MID = 128


learn_rate = 0.1
momentum_coef = 0.9


def shifted(value, axis, steps):
    count = lax.axis_size(axis)
    pairs = [(source, (source + steps) % count) for source in range(count)]
    return lax.ppermute(value, axis, pairs)


def slope(value):
    sig = jax.nn.sigmoid(value)
    return sig * (1.0 + value * (1.0 - sig))


def block_grads(images, cotangent, e_first, e_middle, e_last):
    count, side, _, chans = images.shape
    mid = e_first.shape[1]
    rows = images.reshape(-1, chans)
    cot_rows = cotangent.reshape(-1, chans)
    h_first = jnp.dot(rows, e_first, preferred_element_type=jnp.float32)
    a_first = jax.nn.silu(h_first).astype(jnp.bfloat16)
    padded = jnp.pad(a_first.reshape(count, side, side, mid), ((0, 0), (1, 1), (1, 1), (0, 0)))
    slices = []
    for k_row in range(3):
        for k_col in range(3):
            slices.append(padded[:, k_row : k_row + side, k_col : k_col + side, :].reshape(-1, mid))
    h_middle = jnp.zeros((rows.shape[0], mid), jnp.float32)
    for k in range(9):
        h_middle = h_middle + jnp.dot(
            slices[k], e_middle[k * mid : (k + 1) * mid], preferred_element_type=jnp.float32
        )
    a_middle = jax.nn.silu(h_middle).astype(jnp.bfloat16)
    h_last = jnp.dot(a_middle, e_last, preferred_element_type=jnp.float32)
    pre_out = h_last + rows.astype(jnp.float32)
    d_last = (cot_rows.astype(jnp.float32) * slope(pre_out)).astype(jnp.bfloat16)
    g_last = jnp.einsum("rm,rc->mc", a_middle, d_last, preferred_element_type=jnp.float32)
    da_middle = jnp.einsum("rc,mc->rm", d_last, e_last, preferred_element_type=jnp.float32)
    d_middle = (da_middle * slope(h_middle)).astype(jnp.bfloat16)
    g_parts = []
    back_sum = jnp.zeros((count, side + 2, side + 2, mid), jnp.float32)
    for k in range(9):
        k_row, k_col = (k // 3, k % 3)
        g_parts.append(
            jnp.einsum("rm,rn->mn", slices[k], d_middle, preferred_element_type=jnp.float32)
        )
        term = jnp.einsum(
            "rn,mn->rm",
            d_middle,
            e_middle[k * mid : (k + 1) * mid],
            preferred_element_type=jnp.float32,
        )
        term = term.reshape(count, side, side, mid)
        back_sum = back_sum + jnp.pad(
            term, ((0, 0), (k_row, 2 - k_row), (k_col, 2 - k_col), (0, 0))
        )
    g_middle = jnp.concatenate(g_parts, axis=0)
    da_first = back_sum[:, 1:-1, 1:-1, :].reshape(-1, mid)
    d_first = (da_first * slope(h_first)).astype(jnp.bfloat16)
    g_first = jnp.einsum("rc,rm->cm", rows, d_first, preferred_element_type=jnp.float32)
    return (g_first, g_middle, g_last)


def body(images, cotangent, w_first, w_middle, w_last, m_first, m_middle, m_last):
    scales = (CIN ** (-0.5), (9 * MID) ** (-0.5), MID ** (-0.5))
    weights = [w_first[0], w_middle[0], w_last[0]]
    moments = [m_first[0], m_middle[0], m_last[0]]
    for dist in (1, 2):
        low = tuple(((weights[idx] * scales[idx]).astype(jnp.bfloat16) for idx in range(3)))
        e_first, e_middle, e_last = (
            lax.all_gather(low[0], "dp", axis=0, tiled=True),
            lax.all_gather(low[1], "dp", axis=0, tiled=True),
            lax.all_gather(low[2], "dp", axis=1, tiled=True),
        )
        grads = block_grads(images, cotangent, e_first, e_middle, e_last)
        shares = (
            lax.psum_scatter(grads[0], "dp", scatter_dimension=0, tiled=True),
            lax.psum_scatter(grads[1], "dp", scatter_dimension=0, tiled=True),
            lax.psum_scatter(grads[2], "dp", scatter_dimension=1, tiled=True),
        )
        for idx in range(3):
            moments[idx] = momentum_coef * moments[idx] + scales[idx] * shares[idx]
            weights[idx] = weights[idx] - learn_rate * moments[idx]
        arrived = shifted(
            (weights[0], weights[1], weights[2], moments[0], moments[1], moments[2]), "gossip", dist
        )
        for idx in range(3):
            weights[idx] = 0.5 * (weights[idx] + arrived[idx])
            moments[idx] = 0.5 * (moments[idx] + arrived[idx + 3])
    return (
        weights[0][None],
        weights[1][None],
        weights[2][None],
        moments[0][None],
        moments[1][None],
        moments[2][None],
    )


def solution(mesh):
    in_specs = (
        P(("gossip", "dp"), None, None, None),
        P(("gossip", "dp"), None, None, None),
        P("gossip", "dp", None),
        P("gossip", "dp", None),
        P("gossip", None, "dp"),
        P("gossip", "dp", None),
        P("gossip", "dp", None),
        P("gossip", None, "dp"),
    )
    out_specs = (
        P("gossip", "dp", None),
        P("gossip", "dp", None),
        P("gossip", None, "dp"),
        P("gossip", "dp", None),
        P("gossip", "dp", None),
        P("gossip", None, "dp"),
    )
    return jax.shard_map(body, mesh=mesh, in_specs=in_specs, out_specs=out_specs, check_vma=False)
```

profile of v0, /device:TPU:2, one launch (start us, length us, event | category | flops | bytes accessed | tf_op | source)
XLA Modules:
  0.0 239.2 jit_solution(5783312670260428296)
XLA Ops:
  7.2 1.3 reshape.144
  8.6 6.4 %all_gather.18 = bf16[512,128]{0,1:T(8,128)(2,1)S(1)} all-gather(bf16[256,128]{0,1:T(8,128)(2,1)S(1)} %fusion.6), channel_id=1, replica_groups=mesh['gossip'=128,'dp'=2] {'dp'}, dimensions={0}, use_global_device_ids=true | all-gather | bytes 196608 | tf_op jit(solution)/shard_map/all_gather | solution.py:80
  15.1 1.2 multiply_convert_fusion.7
  17.3 7.3 %all_gather.19 = bf16[1152,128]{1,0:T(8,128)(2,1)S(1)} all-gather(bf16[576,128]{1,0:T(8,128)(2,1)S(1)} %fusion.2), channel_id=1, replica_groups=mesh['gossip'=128,'dp'=2] {'dp'}, dimensions={0}, use_global_device_ids=true | all-gather | bytes 442368 | tf_op jit(solution)/shard_map/all_gather | solution.py:81
  26.4 1.4 reshape.183
  27.7 1.1 fusion.5
  28.8 6.4 %all_gather.20 = bf16[128,512]{1,0:T(8,128)(2,1)S(1)} all-gather(bf16[128,256]{1,0:T(8,128)(2,1)S(1)} %fusion.5), channel_id=1, replica_groups=mesh['gossip'=128,'dp'=2] {'dp'}, dimensions={1}, use_global_device_ids=true | all-gather | bytes 196608 | tf_op jit(solution)/shard_map/all_gather | solution.py:82
  39.7 1.0 fusion.41
  40.7 1.0 fusion.38
  41.8 1.0 fusion.35
  43.0 1.0 reshape.160
  44.0 1.8 reshape.161
  45.8 1.8 reshape.162
  49.9 2.1 convolution_bitcast_fusion.3
  52.2 1.1 fusion.65
  56.9 15.6 %reduce-scatter.7.cloned.1.call-done = f32[256,128]{0,1:T(8,128)} async-done(((f32[512,128]{0,1:T(8,128)}), f32[256,128]{0,1:T(8,128)}) %reduce-scatter.7.cloned.1.call-update) | async-done | bytes 131088 | tf_op jit(solution)/shard_map/reduce_scatter | solution.py:86
  72.6 1.6 bitcast_subtract_fusion.2
  74.1 19.3 %reduce-scatter.11.cloned.1.call-done = f32[128,256]{1,0:T(8,128)} async-done(((f32[128,512]{1,0:T(8,128)}), f32[128,256]{1,0:T(8,128)}) %reduce-scatter.11.cloned.1.call-update) | async-done | bytes 131088 | tf_op jit(solution)/shard_map/reduce_scatter | solution.py:88
  93.5 1.6 bitcast_subtract_fusion.1
  95.2 6.6 %all_gather.21 = bf16[512,128]{0,1:T(8,128)(2,1)S(1)} all-gather(bf16[256,128]{0,1:T(8,128)(2,1)S(1)} %multiply_convert_fusion.12), channel_id=1, replica_groups=mesh['gossip'=128,'dp'=2] {'dp'}, dimensions={0}, use_global_device_ids=true | all-gather | bytes 196608 | tf_op jit(solution)/shard_map/all_gather | solution.py:80
  101.8 1.1 multiply_convert_fusion.4
  103.0 14.4 %reduce-scatter.9.cloned.1.call-done = f32[576,128]{1,0:T(8,128)} async-done(((f32[1152,128]{1,0:T(8,128)}), f32[576,128]{1,0:T(8,128)}) %reduce-scatter.9.cloned.1.call-update) | async-done | bytes 294928 | tf_op jit(solution)/shard_map/reduce_scatter | solution.py:87
  117.4 1.8 bitcast_subtract_fusion
  119.2 1.0 pad_slice_fusion
  120.1 1.0 reshape.165
  121.5 6.4 %all_gather.23 = bf16[128,512]{1,0:T(8,128)(2,1)S(1)} all-gather(bf16[128,256]{1,0:T(8,128)(2,1)S(1)} %multiply_convert_fusion.11), channel_id=1, replica_groups=mesh['gossip'=128,'dp'=2] {'dp'}, dimensions={1}, use_global_device_ids=true | all-gather | bytes 196608 | tf_op jit(solution)/shard_map/all_gather | solution.py:82
  128.0 1.6 collective-permute-done.2
  129.7 7.3 %all_gather.22 = bf16[1152,128]{1,0:T(8,128)(2,1)S(1)} all-gather(bf16[576,128]{1,0:T(8,128)(2,1)S(1)} %multiply_convert_fusion.8), channel_id=1, replica_groups=mesh['gossip'=128,'dp'=2] {'dp'}, dimensions={0}, use_global_device_ids=true | all-gather | bytes 442368 | tf_op jit(solution)/shard_map/all_gather | solution.py:81
  141.0 1.1 fusion.66
  142.5 0.9 convolution_dynamic-update-slice_fusion.8
  143.3 1.0 fusion.31
  145.4 1.0 fusion.16
  146.5 1.0 fusion.13
  147.5 1.0 fusion.10
  148.5 1.0 fusion.7
  149.6 0.9 convolution_dynamic-update-slice_fusion.7
  150.5 0.9 convolution_dynamic-update-slice_fusion.6
  151.4 0.9 convolution_dynamic-update-slice_fusion.5
  152.3 1.0 reshape.173
  153.5 1.0 reshape.178
  154.5 1.8 reshape.179
  156.3 1.8 reshape.180
  158.1 1.8 reshape.181
  162.2 0.9 convolution_dynamic-update-slice_fusion.4
  163.1 0.9 convolution_dynamic-update-slice_fusion.3
  164.0 1.1 convolution_bitcast_fusion.2
  165.3 0.9 convolution_dynamic-update-slice_fusion.2
  166.2 0.9 convolution_dynamic-update-slice_fusion.1
  167.0 0.9 convolution_dynamic-update-slice_fusion
  168.1 1.1 collective-permute-start.1
  169.3 7.4 %collective-permute-done.7 = f32[128,256]{1,0:T(8,128)S(1)} collective-permute-done((f32[128,256]{1,0:T(8,128)S(1)}, f32[128,256]{1,0:T(8,128)S(1)}, u32[]{:S(2)}, u32[]{:S(2)}) %collective-permute-start.7) | collective-permute-done | bytes 131104 | tf_op jit(solution)/shard_map/ppermute | solution.py:17
  176.7 1.0 multiply_subtract_fusion.1
  178.1 8.8 %reduce-scatter.13.cloned.1.call-done = f32[256,128]{0,1:T(8,128)} async-done(((f32[512,128]{0,1:T(8,128)}), f32[256,128]{0,1:T(8,128)}) %reduce-scatter.13.cloned.1.call-update) | async-done | bytes 131088 | tf_op jit(solution)/shard_map/reduce_scatter | solution.py:86
  186.9 1.0 multiply_subtract_fusion.2
  187.9 1.6 collective-permute-start.9
  189.5 1.5 collective-permute-start.8
  191.0 1.6 collective-permute-start.4
  193.3 5.3 %collective-permute-done.9 = f32[256,128]{0,1:T(8,128)S(1)} collective-permute-done((f32[256,128]{0,1:T(8,128)S(1)}, f32[256,128]{0,1:T(8,128)S(1)}, u32[]{:S(2)}, u32[]{:S(2)}) %collective-permute-start.9) | collective-permute-done | bytes 131104 | tf_op jit(solution)/shard_map/ppermute | solution.py:17
  198.6 12.1 %reduce-scatter.15.cloned.1.call-done = f32[576,128]{1,0:T(8,128)} async-done(((f32[1152,128]{1,0:T(8,128)}), f32[576,128]{1,0:T(8,128)}) %reduce-scatter.15.cloned.1.call-update) | async-done | bytes 294928 | tf_op jit(solution)/shard_map/reduce_scatter | solution.py:87
  210.8 1.1 multiply_subtract_fusion
  211.9 1.6 collective-permute-start.10
  214.1 1.6 collective-permute-start.6
  217.3 8.9 %collective-permute-done.10 = f32[576,128]{1,0:T(8,128)S(1)} collective-permute-done((f32[576,128]{1,0:T(8,128)S(1)}, f32[576,128]{1,0:T(8,128)S(1)}, u32[]{:S(2)}, u32[]{:S(2)}) %collective-permute-start.10) | collective-permute-done | bytes 294944 | tf_op jit(solution)/shard_map/ppermute | solution.py:17
  226.9 4.7 %collective-permute-done.6 = f32[576,128]{1,0:T(8,128)S(1)} collective-permute-done((f32[576,128]{1,0:T(8,128)S(1)}, f32[576,128]{1,0:T(8,128)S(1)}, u32[]{:S(2)}, u32[]{:S(2)}) %collective-permute-start.6) | collective-permute-done | bytes 294944 | tf_op jit(solution)/shard_map/ppermute | solution.py:17
  (250 shorter events, 26.4 us)
Async XLA Ops:
  7.2 65.4 %reduce-scatter.7.cloned.1.call-start = ((), (), s32[]{:S(2)}) async-start(), calls=%async_computation.6 | async-start | bytes 393216 | tf_op jit(solution)/shard_map/reduce_scatter | solution.py:86
  8.5 6.6 %copy-start.44 = (bf16[784,512]{1,0:T(8,128)(2,1)}, bf16[784,512]{1,0:T(8,128)(2,1)S(1)}, u32[]{:S(2)}) copy-start(bf16[784,512]{1,0:T(8,128)(2,1)S(1)} %reshape.144) | copy-start | bytes 2408452
  16.2 9.6 %copy-start.9 = (bf16[784,128]{1,0:T(8,128)(2,1)}, bf16[784,128]{1,0:T(8,128)(2,1)S(1)}, u32[]{:S(2)}) copy-start(bf16[784,128]{1,0:T(8,128)(2,1)S(1)} %get-tuple-element.46) | copy-start | bytes 602116
  17.3 8.0 %copy-start.5 = (bf16[784,128]{1,0:T(8,128)(2,1)}, bf16[784,128]{1,0:T(8,128)(2,1)S(1)}, u32[]{:S(2)}) copy-start(bf16[784,128]{1,0:T(8,128)(2,1)S(1)} %reshape.146) | copy-start | bytes 602116
  26.2 9.1 %copy-start.31 = (bf16[784,128]{1,0:T(8,128)(2,1)}, bf16[784,128]{1,0:T(8,128)(2,1)S(1)}, u32[]{:S(2)}) copy-start(bf16[784,128]{1,0:T(8,128)(2,1)S(1)} %reshape.150) | copy-start | bytes 602116
  26.2 9.3 %copy-start.29 = (bf16[784,128]{1,0:T(8,128)(2,1)}, bf16[784,128]{1,0:T(8,128)(2,1)S(1)}, u32[]{:S(2)}) copy-start(bf16[784,128]{1,0:T(8,128)(2,1)S(1)} %reshape.151) | copy-start | bytes 602116
  26.3 9.5 %copy-start.25 = (bf16[784,128]{1,0:T(8,128)(2,1)}, bf16[784,128]{1,0:T(8,128)(2,1)S(1)}, u32[]{:S(2)}) copy-start(bf16[784,128]{1,0:T(8,128)(2,1)S(1)} %reshape.152) | copy-start | bytes 602116
  26.3 9.7 %copy-start.27 = (bf16[784,128]{1,0:T(8,128)(2,1)}, bf16[784,128]{1,0:T(8,128)(2,1)S(1)}, u32[]{:S(2)}) copy-start(bf16[784,128]{1,0:T(8,128)(2,1)S(1)} %reshape.153) | copy-start | bytes 602116
  27.7 8.5 %copy-start.33 = (f32[784,512]{1,0:T(8,128)}, f32[784,512]{1,0:T(8,128)S(1)}, u32[]{:S(2)}) copy-start(f32[784,512]{1,0:T(8,128)S(1)} %reshape.183) | copy-start | bytes 4816900
  49.2 2.9 %copy-start.59 = (f32[784,128]{1,0:T(8,128)S(1)}, f32[784,128]{1,0:T(8,128)}, u32[]{:S(2)}) copy-start(f32[784,128]{1,0:T(8,128)} %copy-done.58) | copy-start | bytes 1204228
  49.2 2.9 %copy-start.65 = (bf16[784,512]{1,0:T(8,128)(2,1)S(1)}, bf16[784,512]{1,0:T(8,128)(2,1)}, u32[]{:S(2)}) copy-start(bf16[784,512]{1,0:T(8,128)(2,1)} %copy-done.64) | copy-start | bytes 2408452
  52.1 1.8 copy-start.20
  52.1 2.1 copy-start.18
  52.1 41.4 %reduce-scatter.11.cloned.1.call-start = ((), (), s32[]{:S(2)}) async-start(), calls=%async_computation.8 | async-start | bytes 393216 | tf_op jit(solution)/shard_map/reduce_scatter | solution.py:88
  53.2 1.8 copy-start.30
  53.3 2.1 copy-start.26
  53.3 64.1 %reduce-scatter.9.cloned.1.call-start = ((), (), s32[]{:S(2)}) async-start(), calls=%async_computation.7 | async-start | bytes 884736 | tf_op jit(solution)/shard_map/reduce_scatter | solution.py:87
  53.6 2.0 copy-start.28
  54.2 2.6 %copy-start.63 = (f32[1,256,128]{2,1,0:T(8,128)S(1)}, f32[1,256,128]{2,1,0:T(8,128)}, u32[]{:S(2)}) copy-start(f32[1,256,128]{2,1,0:T(8,128)} %param.13) | copy-start | bytes 393220
  54.8 38.7 %copy-start.53 = (f32[1,128,256]{2,1,0:T(8,128)S(1)}, f32[1,128,256]{2,1,0:T(8,128)}, u32[]{:S(2)}) copy-start(f32[1,128,256]{2,1,0:T(8,128)} %param.12) | copy-start | bytes 393220
  54.8 38.7 %copy-start.61 = (f32[1,128,256]{2,1,0:T(8,128)S(1)}, f32[1,128,256]{2,1,0:T(8,128)}, u32[]{:S(2)}) copy-start(f32[1,128,256]{2,1,0:T(8,128)} %param.15) | copy-start | bytes 393220
  55.6 46.2 %copy-start.47 = (bf16[784,512]{1,0:T(8,128)(2,1)S(1)}, bf16[784,512]{1,0:T(8,128)(2,1)}, u32[]{:S(2)}) copy-start(bf16[784,512]{1,0:T(8,128)(2,1)} %copy-done.44) | copy-start | bytes 2408452
  56.7 119.9 %reduce-scatter.17.cloned.1.call-start = ((), (), s32[]{:S(2)}) async-start(), calls=%async_computation.11 | async-start | bytes 393216 | tf_op jit(solution)/shard_map/reduce_scatter | solution.py:88
  74.1 28.8 %copy-start.35 = (f32[256,128]{0,1:T(8,128)}, f32[256,128]{0,1:T(8,128)S(1)}, u32[]{:S(2)}) copy-start(f32[256,128]{0,1:T(8,128)S(1)} %get-tuple-element.26) | copy-start | bytes 393220
  74.1 20.9 %collective-permute-start = (f32[256,128]{0,1:T(8,128)S(1)}, f32[256,128]{0,1:T(8,128)S(1)}, u32[]{:S(2)}, u32[]{:S(2)}) collective-permute-start(f32[256,128]{0,1:T(8,128)S(1)} %get-tuple-element.26), channel_id=1, source_target_pairs={{0,2},{2,4},{4,6},{6,8},{8,10},{10,12},{12,14},{14,16},{16,18},{18... | collective-permute-start | bytes 393224 | tf_op jit(solution)/shard_map/ppermute | solution.py:17
  95.1 26.4 %copy-start.37 = (f32[128,256]{1,0:T(8,128)}, f32[128,256]{1,0:T(8,128)S(1)}, u32[]{:S(2)}) copy-start(f32[128,256]{1,0:T(8,128)S(1)} %get-tuple-element.28) | copy-start | bytes 393220
  95.1 26.4 %collective-permute-start.3 = (f32[128,256]{1,0:T(8,128)S(1)}, f32[128,256]{1,0:T(8,128)S(1)}, u32[]{:S(2)}, u32[]{:S(2)}) collective-permute-start(f32[128,256]{1,0:T(8,128)S(1)} %get-tuple-element.28), channel_id=1, source_target_pairs={{0,2},{2,4},{4,6},{6,8},{8,10},{10,12},{12,14},{14,16},{16,18},{18... | collective-permute-start | bytes 393224 | tf_op jit(solution)/shard_map/ppermute | solution.py:17
  95.1 7.9 %copy-start.54 = (f32[256,128]{0,1:T(8,128)}, f32[256,128]{0,1:T(8,128)S(1)}, u32[]{:S(2)}) copy-start(f32[256,128]{0,1:T(8,128)S(1)} %collective-permute-done) | copy-start | bytes 393220
  95.1 22.2 %copy-start.40 = (f32[1,576,128]{2,1,0:T(8,128)S(1)}, f32[1,576,128]{2,1,0:T(8,128)}, u32[]{:S(2)}) copy-start(f32[1,576,128]{2,1,0:T(8,128)} %param.11) | copy-start | bytes 884740
  95.1 22.2 %copy-start.60 = (f32[1,576,128]{2,1,0:T(8,128)S(1)}, f32[1,576,128]{2,1,0:T(8,128)}, u32[]{:S(2)}) copy-start(f32[1,576,128]{2,1,0:T(8,128)} %param.14) | copy-start | bytes 884740
  103.0 35.1 %copy-start.7 = (bf16[784,128]{1,0:T(8,128)(2,1)}, bf16[784,128]{1,0:T(8,128)(2,1)S(1)}, u32[]{:S(2)}) copy-start(bf16[784,128]{1,0:T(8,128)(2,1)S(1)} %get-tuple-element.48) | copy-start | bytes 602116
  119.1 10.5 %collective-permute-start.2 = (f32[576,128]{1,0:T(8,128)S(1)}, f32[576,128]{1,0:T(8,128)S(1)}, u32[]{:S(2)}, u32[]{:S(2)}) collective-permute-start(f32[576,128]{1,0:T(8,128)S(1)} %get-tuple-element.24), channel_id=1, source_target_pairs={{0,2},{2,4},{4,6},{6,8},{8,10},{10,12},{12,14},{14,16},{16,18},{18... | collective-permute-start | bytes 884744 | tf_op jit(solution)/shard_map/ppermute | solution.py:17
  121.3 17.0 %copy-start.21 = (bf16[784,128]{1,0:T(8,128)(2,1)}, bf16[784,128]{1,0:T(8,128)(2,1)S(1)}, u32[]{:S(2)}) copy-start(bf16[784,128]{1,0:T(8,128)(2,1)S(1)} %reshape.169) | copy-start | bytes 602116
  121.4 17.2 %copy-start.15 = (bf16[784,128]{1,0:T(8,128)(2,1)}, bf16[784,128]{1,0:T(8,128)(2,1)S(1)}, u32[]{:S(2)}) copy-start(bf16[784,128]{1,0:T(8,128)(2,1)S(1)} %reshape.170) | copy-start | bytes 602116
  121.4 17.4 %copy-start.11 = (bf16[784,128]{1,0:T(8,128)(2,1)}, bf16[784,128]{1,0:T(8,128)(2,1)S(1)}, u32[]{:S(2)}) copy-start(bf16[784,128]{1,0:T(8,128)(2,1)S(1)} %reshape.171) | copy-start | bytes 602116
  121.5 17.6 %copy-start.13 = (bf16[784,128]{1,0:T(8,128)(2,1)}, bf16[784,128]{1,0:T(8,128)(2,1)S(1)}, u32[]{:S(2)}) copy-start(bf16[784,128]{1,0:T(8,128)(2,1)S(1)} %reshape.172) | copy-start | bytes 602116
  121.5 16.0 %copy-start.56 = (f32[128,256]{1,0:T(8,128)}, f32[128,256]{1,0:T(8,128)S(1)}, u32[]{:S(2)}) copy-start(f32[128,256]{1,0:T(8,128)S(1)} %collective-permute-done.3) | copy-start | bytes 393220
  129.6 8.2 %copy-start.42 = (f32[576,128]{1,0:T(8,128)}, f32[576,128]{1,0:T(8,128)S(1)}, u32[]{:S(2)}) copy-start(f32[576,128]{1,0:T(8,128)S(1)} %collective-permute-done.2) | copy-start | bytes 884740
  138.6 1.6 copy-start.48
  149.6 37.3 %reduce-scatter.13.cloned.1.call-start = ((), (), s32[]{:S(2)}) async-start(), calls=%async_computation.9 | async-start | bytes 393216 | tf_op jit(solution)/shard_map/reduce_scatter | solution.py:86
  161.3 1.8 copy-start.22
  162.2 1.8 copy-start.49
  162.2 1.8 copy-start.66
  163.1 2.2 copy-start.16
  164.0 2.1 copy-start.12
  164.0 3.0 %copy-start.14 = (bf16[784,128]{1,0:T(8,128)(2,1)S(1)}, bf16[784,128]{1,0:T(8,128)(2,1)}, u32[]{:S(2)}) copy-start(bf16[784,128]{1,0:T(8,128)(2,1)} %copy-done.13) | copy-start | bytes 602116
  165.2 2.8 %copy-start.52 = (f32[128,256]{1,0:T(8,128)S(1)}, f32[128,256]{1,0:T(8,128)}, u32[]{:S(2)}) copy-start(f32[128,256]{1,0:T(8,128)} %get-tuple-element.29) | copy-start | bytes 393220
  165.2 2.9 %copy-start.51 = (f32[256,128]{0,1:T(8,128)S(1)}, f32[256,128]{0,1:T(8,128)}, u32[]{:S(2)}) copy-start(f32[256,128]{0,1:T(8,128)} %get-tuple-element.27) | copy-start | bytes 393220
  165.2 4.0 %copy-start.41 = (f32[576,128]{1,0:T(8,128)S(1)}, f32[576,128]{1,0:T(8,128)}, u32[]{:S(2)}) copy-start(f32[576,128]{1,0:T(8,128)} %get-tuple-element.25) | copy-start | bytes 884740
  165.2 11.5 %copy-start.38 = (f32[128,256]{1,0:T(8,128)S(1)}, f32[128,256]{1,0:T(8,128)}, u32[]{:S(2)}) copy-start(f32[128,256]{1,0:T(8,128)} %copy-done.37) | copy-start | bytes 393220
  165.2 11.5 %copy-start.57 = (f32[128,256]{1,0:T(8,128)S(1)}, f32[128,256]{1,0:T(8,128)}, u32[]{:S(2)}) copy-start(f32[128,256]{1,0:T(8,128)} %copy-done.56) | copy-start | bytes 393220
  165.2 21.7 %copy-start.36 = (f32[256,128]{0,1:T(8,128)S(1)}, f32[256,128]{0,1:T(8,128)}, u32[]{:S(2)}) copy-start(f32[256,128]{0,1:T(8,128)} %copy-done.35) | copy-start | bytes 393220
  165.2 21.7 %copy-start.55 = (f32[256,128]{0,1:T(8,128)S(1)}, f32[256,128]{0,1:T(8,128)}, u32[]{:S(2)}) copy-start(f32[256,128]{0,1:T(8,128)} %copy-done.54) | copy-start | bytes 393220
  165.2 45.6 %reduce-scatter.15.cloned.1.call-start = ((), (), s32[]{:S(2)}) async-start(), calls=%async_computation.10 | async-start | bytes 884736 | tf_op jit(solution)/shard_map/reduce_scatter | solution.py:87
  167.9 42.9 %copy-start.43 = (f32[576,128]{1,0:T(8,128)S(1)}, f32[576,128]{1,0:T(8,128)}, u32[]{:S(2)}) copy-start(f32[576,128]{1,0:T(8,128)} %copy-done.42) | copy-start | bytes 884740
  168.0 8.7 %collective-permute-start.7 = (f32[128,256]{1,0:T(8,128)S(1)}, f32[128,256]{1,0:T(8,128)S(1)}, u32[]{:S(2)}, u32[]{:S(2)}) collective-permute-start(f32[128,256]{1,0:T(8,128)S(1)} %copy-done.52), channel_id=1, source_target_pairs={{0,2},{2,4},{4,6},{6,8},{8,10},{10,12},{12,14},{14,16},{16,18},{18... | collective-permute-start | bytes 393224 | tf_op jit(solution)/shard_map/ppermute | solution.py:17
  168.1 10.0 %collective-permute-start.1 = (f32[256,128]{0,1:T(8,128)S(1)}, f32[256,128]{0,1:T(8,128)S(1)}, u32[]{:S(2)}, u32[]{:S(2)}) collective-permute-start(f32[256,128]{0,1:T(8,128)S(1)} %copy-done.51), channel_id=1, source_target_pairs={{0,2},{2,4},{4,6},{6,8},{8,10},{10,12},{12,14},{14,16},{16,18},{18... | collective-permute-start | bytes 393224 | tf_op jit(solution)/shard_map/ppermute | solution.py:17
  169.2 29.5 %collective-permute-start.5 = (f32[576,128]{1,0:T(8,128)S(1)}, f32[576,128]{1,0:T(8,128)S(1)}, u32[]{:S(2)}, u32[]{:S(2)}) collective-permute-start(f32[576,128]{1,0:T(8,128)S(1)} %copy-done.41), channel_id=1, source_target_pairs={{0,2},{2,4},{4,6},{6,8},{8,10},{10,12},{12,14},{14,16},{16,18},{18... | collective-permute-start | bytes 884744 | tf_op jit(solution)/shard_map/ppermute | solution.py:17
  177.6 15.0 %collective-permute-start.11 = (f32[128,256]{1,0:T(8,128)S(1)}, f32[128,256]{1,0:T(8,128)S(1)}, u32[]{:S(2)}, u32[]{:S(2)}) collective-permute-start(f32[128,256]{1,0:T(8,128)S(1)} %get-tuple-element.19), channel_id=1, source_target_pairs={{0,4},{2,6},{4,8},{6,10},{8,12},{10,14},{12,16},{14,18},{16,20},{1... | collective-permute-start | bytes 393224 | tf_op jit(solution)/shard_map/ppermute | solution.py:17
  187.9 10.8 %collective-permute-start.9 = (f32[256,128]{0,1:T(8,128)S(1)}, f32[256,128]{0,1:T(8,128)S(1)}, u32[]{:S(2)}, u32[]{:S(2)}) collective-permute-start(f32[256,128]{0,1:T(8,128)S(1)} %get-tuple-element.23), channel_id=1, source_target_pairs={{0,4},{2,6},{4,8},{6,10},{8,12},{10,14},{12,16},{14,18},{16,20},{1... | collective-permute-start | bytes 393224 | tf_op jit(solution)/shard_map/ppermute | solution.py:17
  189.5 24.0 %collective-permute-start.8 = (f32[128,256]{1,0:T(8,128)S(1)}, f32[128,256]{1,0:T(8,128)S(1)}, u32[]{:S(2)}, u32[]{:S(2)}) collective-permute-start(f32[128,256]{1,0:T(8,128)S(1)} %get-tuple-element.18), channel_id=1, source_target_pairs={{0,4},{2,6},{4,8},{6,10},{8,12},{10,14},{12,16},{14,18},{16,20},{1... | collective-permute-start | bytes 393224 | tf_op jit(solution)/shard_map/ppermute | solution.py:17
  191.0 24.7 %collective-permute-start.4 = (f32[256,128]{0,1:T(8,128)S(1)}, f32[256,128]{0,1:T(8,128)S(1)}, u32[]{:S(2)}, u32[]{:S(2)}) collective-permute-start(f32[256,128]{0,1:T(8,128)S(1)} %get-tuple-element.22), channel_id=1, source_target_pairs={{0,4},{2,6},{4,8},{6,10},{8,12},{10,14},{12,16},{14,18},{16,20},{1... | collective-permute-start | bytes 393224 | tf_op jit(solution)/shard_map/ppermute | solution.py:17
  211.9 14.3 %collective-permute-start.10 = (f32[576,128]{1,0:T(8,128)S(1)}, f32[576,128]{1,0:T(8,128)S(1)}, u32[]{:S(2)}, u32[]{:S(2)}) collective-permute-start(f32[576,128]{1,0:T(8,128)S(1)} %get-tuple-element.21), channel_id=1, source_target_pairs={{0,4},{2,6},{4,8},{6,10},{8,12},{10,14},{12,16},{14,18},{16,20},{1... | collective-permute-start | bytes 884744 | tf_op jit(solution)/shard_map/ppermute | solution.py:17
  214.1 17.5 %collective-permute-start.6 = (f32[576,128]{1,0:T(8,128)S(1)}, f32[576,128]{1,0:T(8,128)S(1)}, u32[]{:S(2)}, u32[]{:S(2)}) collective-permute-start(f32[576,128]{1,0:T(8,128)S(1)} %get-tuple-element.20), channel_id=1, source_target_pairs={{0,4},{2,6},{4,8},{6,10},{8,12},{10,14},{12,16},{14,18},{16,20},{1... | collective-permute-start | bytes 884744 | tf_op jit(solution)/shard_map/ppermute | solution.py:17
  (21 other events, 23.9 us)
Sparse Core Ops, SparseCore 0:
  52.2 20.2 reduce-scatter.6
  75.8 17.6 reduce-scatter.10
  96.0 21.3 reduce-scatter.8
  149.7 17.0 reduce-scatter.16
  169.1 17.7 reduce-scatter.12
  189.4 21.3 reduce-scatter.14
where the time goes:
time: 241 us; the launch traced here: 239 us
  waiting for transfers between devices  98.8 us (41%)
  blocking collectives  40.6 us (17%)
  matrix products  35.5 us (15%)
  local copies, waits for them, and re-layouts  26.2 us (11%)
  between operations  15.4 us (6%)
  other arithmetic  13.2 us (5%)
  starting transfers between devices  9.53 us (4%)
    ppermute x12, waiting for transfers between devices, shifted(): return lax.ppermute(value, axis, pairs)  28.4 us
    reduce_scatter x2, waiting for transfers between devices, body(): lax.psum_scatter(grads[1], 'dp', scatter_dimension=0, tiled=True)  26.5 us
    reduce_scatter x2, waiting for transfers between devices, body(): lax.psum_scatter(grads[0], 'dp', scatter_dimension=0, tiled=True)  24.5 us
    reduce_scatter x2, waiting for transfers between devices, body(): lax.psum_scatter(grads[2], 'dp', scatter_dimension=1, tiled=True)  19.3 us
    all_gather x2, blocking collectives, body(): lax.all_gather(low[1], 'dp', axis=0, tiled=True)  14.6 us
    all_gather x2, blocking collectives, body(): lax.all_gather(low[0], 'dp', axis=0, tiled=True)  13.1 us
    all_gather x2, blocking collectives, body(): lax.all_gather(low[2], 'dp', axis=1, tiled=True)  12.9 us
    reshape x18, local copies, waits for them, and re-layouts, block_grads(): term = term.reshape(count, side, side, mid)  12.4 us
  transfers between devices with their start and end apart: 18, of which 11 were waited for; matrix products, arithmetic and copies ran while one was open for 15% of the time, Pallas kernels for 0%

commit v1 on v0

v1 whole, which is shorter than its diff:
```python
import functools

import jax
import jax.numpy as jnp
from jax import lax
from jax.experimental import pallas as pl
from jax.experimental.pallas import tpu as pltpu
from jax.sharding import PartitionSpec as P

CIN = 512
MID = 128
SIDE = 28
PITCH = 32
ROWS = SIDE * PITCH
BF16 = jnp.bfloat16
F32 = jnp.float32
MESH = pl.DeviceIdType.MESH
SCALES = (CIN ** (-0.5), (9 * MID) ** (-0.5), MID ** (-0.5))
SHARDS = ((256, 128), (576, 128), (128, 256))
FULLS = ((512, 128), (1152, 128), (128, 512))
learn_rate = 0.1
momentum_coef = 0.9

CHUNKS = ((0, 0, 256), (1, 0, 192), (1, 192, 192), (1, 384, 192), (2, 0, 128))
N_CHUNKS = len(CHUNKS)
E, W, G, M = range(4)


def sigmoid(v):
    return 0.5 * jnp.tanh(0.5 * v) + 0.5


def dot(a, b):
    return jnp.dot(a, b, preferred_element_type=F32)


def dot_nt(a, b):
    return lax.dot_general(a, b, (((1,), (1,)), ((), ())), preferred_element_type=F32)


def half(idx, ref, which, row, rows):
    if idx == 2:
        return ref.at[pl.ds(row, rows), pl.ds(pl.multiple_of(which * 256, 256), 256)]
    start = pl.multiple_of(which * SHARDS[idx][0] + row, 16)
    return ref.at[pl.ds(start, rows), :]


def pad_pixels(src, dst):
    dst[...] = jnp.zeros_like(dst)
    for i in range(SIDE):
        dst[pl.ds(i * PITCH, SIDE), :] = src[i]


def kernel(*refs):
    images, cotangent = refs[0:2]
    w_in, m_in = refs[2:5], refs[5:8]
    w_out, m_out = refs[8:11], refs[11:14]
    (
        x_raw, c_raw, x, xt, cot, e2f, e2r, a1s, d2s, a1t, a2, slope1, slope2, d3,
        w1, w2, w3, m1, m2, m3, g1, g2, g3,
        e1, e2, e3, wb1, wb2, wb3, wa1, wa2, wa3, gb1, gb2, gb3, ga1, ga2, ga3,
        mb1, mb2, mb3, ma1, ma2, ma3, send_sem, recv_sem, in_sem,
    ) = refs[14:]
    w, m, g, e = (w1, w2, w3), (m1, m2, m3), (g1, g2, g3), (e1, e2, e3)
    wb, wa, gb, ga, mb, ma = (
        (wb1, wb2, wb3), (wa1, wa2, wa3), (gb1, gb2, gb3), (ga1, ga2, ga3),
        (mb1, mb2, mb3), (ma1, ma2, ma3),
    )
    me, dp = lax.axis_index("gossip"), lax.axis_index("dp")
    count = lax.axis_size("gossip")

    def at(steps):
        return (lax.rem(me + steps + count, count), dp)

    partner = (me, 1 - dp)

    barrier = pltpu.get_barrier_semaphore()
    for other in (partner, at(1), at(-1), at(2), at(-2)):
        pl.semaphore_signal(barrier, inc=1, device_id=other, device_id_type=MESH)

    loads = {}
    for n, (src, dst) in enumerate(
        list(zip(w_in, w)) + [(images, x_raw), (cotangent, c_raw)] + list(zip(m_in, m))
    ):
        loads[n] = pltpu.make_async_copy(src, dst, in_sem.at[n])
        loads[n].start()

    def remote(kind, it, k):
        idx, row, rows = CHUNKS[k]
        rs = pl.ds(row, rows)
        if kind == E:
            src = half(idx, e[idx].at[it], dp, row, rows)
            dst, to = src, partner
        elif kind == W:
            src, dst, to = wb[idx].at[it, rs, :], wa[idx].at[it, rs, :], at(it + 1)
        elif kind == G:
            src, dst, to = gb[idx].at[it, rs, :], ga[idx].at[it, rs, :], partner
        else:
            src, dst, to = mb[idx].at[it, rs, :], ma[idx].at[it, rs, :], at(it + 1)
        return pltpu.make_async_remote_copy(
            src_ref=src, dst_ref=dst, send_sem=send_sem.at[kind, it, k],
            recv_sem=recv_sem.at[kind, it, k], device_id=to, device_id_type=MESH,
        )

    def of(idx):
        return [k for k in range(N_CHUNKS) if CHUNKS[k][0] == idx]

    for idx in range(3):
        loads[idx].wait()
        full = (0, SHARDS[idx][0])
        half(idx, e[idx].at[0], dp, *full)[...] = (w[idx][...] * SCALES[idx]).astype(BF16)
        wb[idx][0] = w[idx][...].astype(BF16)
    pl.semaphore_wait(barrier, 5)
    for k in range(N_CHUNKS):
        remote(E, 0, k).start()

    d2s[...] = jnp.zeros_like(d2s)
    loads[3].wait()
    pad_pixels(x_raw, x)
    xt[...] = x[...].T
    loads[4].wait()
    pad_pixels(c_raw, cot)
    for n in range(5, 8):
        loads[n].wait()

    zero = jnp.zeros((PITCH, MID), F32)

    def take(it, k):
        idx, row, rows = CHUNKS[k]
        rs = pl.ds(row, rows)
        remote(G, it, k).wait_recv()
        total = half(idx, g[idx], dp, row, rows)[...] + ga[idx][it, rs, :].astype(F32)
        new = momentum_coef * m[idx][rs, :] + SCALES[idx] * total
        m[idx][rs, :] = new
        mb[idx][it, rs, :] = new.astype(BF16)
        remote(M, it, k).start()

    def mix(it, k):
        idx, row, rows = CHUNKS[k]
        rs = pl.ds(row, rows)
        remote(M, it, k).wait_recv()
        mean = 0.5 * (m[idx][rs, :] + ma[idx][it, rs, :].astype(F32))
        if it == 0:
            remote(W, it, k).wait_recv()
        weight = 0.5 * (w[idx][rs, :] + wa[idx][it, rs, :].astype(F32)) - learn_rate * mean
        if it == 0:
            m[idx][rs, :] = mean
            w[idx][rs, :] = weight
            half(idx, e[idx].at[1], dp, row, rows)[...] = (weight * SCALES[idx]).astype(BF16)
            remote(E, 1, k).start()
            wb[idx][1, rs, :] = weight.astype(BF16)
            remote(W, 1, k).start()
        else:
            m_out[idx][rs, :] = mean
            w_out[idx][rs, :] = weight

    def send_grad(it, idx):
        for k in of(idx):
            _, row, rows = CHUNKS[k]
            gb[idx][it, pl.ds(row, rows), :] = half(idx, g[idx], 1 - dp, row, rows)[...].astype(BF16)
            remote(G, it, k).start()

    for it in range(2):
        for k in of(0):
            remote(E, it, k).wait_recv()
        h1 = dot(x[...], e1[it])
        sig = sigmoid(h1)
        act1 = h1 * sig
        slope1[...] = sig * (1.0 + h1 * (1.0 - sig))
        a1s[:, 0:128] = pltpu.roll(act1, 1, 0).astype(BF16)
        a1s[:, 128:256] = act1.astype(BF16)
        a1s[:, 256:384] = pltpu.roll(act1, ROWS - 1, 0).astype(BF16)
        a1t[...] = act1.astype(BF16).T
        for k in of(1):
            remote(E, it, k).wait_recv()
        for ky in range(3):
            e2f[:, ky * 128 : (ky + 1) * 128] = e2[it, pl.ds(ky * 384, 384), :]
            for kx in range(3):
                e2r[pl.ds(ky * 128, 128), kx * 128 : (kx + 1) * 128] = e2[
                    it, pl.ds((3 * ky + kx) * 128, 128), :
                ]
        u = dot(a1s[...], e2f[...])
        h2 = (
            u[:, 128:256]
            + jnp.concatenate([zero, u[: ROWS - PITCH, 0:128]], axis=0)
            + jnp.concatenate([u[PITCH:, 256:384], zero], axis=0)
        )
        sig = sigmoid(h2)
        slope2[...] = sig * (1.0 + h2 * (1.0 - sig))
        a2[...] = (h2 * sig).astype(BF16)
        for k in of(2):
            remote(E, it, k).wait_recv()
        if it == 0:
            for k in range(N_CHUNKS):
                remote(W, 0, k).start()
        for j in range(7):
            rs = pl.ds(j * 128, 128)
            pre = dot(a2[rs, :], e3[it]) + x[rs, :].astype(F32)
            sig = sigmoid(pre)
            d3[rs, :] = (cot[rs, :].astype(F32) * (sig * (1.0 + pre * (1.0 - sig)))).astype(BF16)
        if it == 1:
            g3[...] = dot(a2[...].T, d3[...])
            send_grad(it, 2)
        d2 = dot_nt(d3[...], e3[it]) * slope2[...]
        inner = pl.ds(PITCH, ROWS)
        d2s[inner, 0:128] = pltpu.roll(d2, ROWS - 1, 0).astype(BF16)
        d2s[inner, 128:256] = d2.astype(BF16)
        d2s[inner, 256:384] = pltpu.roll(d2, 1, 0).astype(BF16)

        def first():
            t = dot_nt(d2s[inner, :], e2r[...])
            da1 = (
                t[:, 128:256]
                + jnp.concatenate([t[PITCH:, 0:128], zero], axis=0)
                + jnp.concatenate([zero, t[: ROWS - PITCH, 256:384]], axis=0)
            )
            d1 = (da1 * slope1[...]).astype(BF16)
            g1[...] = dot(xt[...], d1)
            send_grad(it, 0)

        def middle():
            for ky in range(3):
                gk = dot(a1t[...], d2s[pl.ds((2 - ky) * PITCH, ROWS), :])
                for kx in range(3):
                    g2[pl.ds((3 * ky + kx) * 128, 128), :] = gk[:, kx * 128 : (kx + 1) * 128]
            send_grad(it, 1)

        if it == 0:
            first()
            middle()
            g3[...] = dot(a2[...].T, d3[...])
            send_grad(it, 2)
            order = (0, 1, 2, 3, 4)
        else:
            middle()
            first()
            for k in range(N_CHUNKS):
                remote(W, 1, k).wait_recv()
            order = (4, 1, 2, 3, 0)
        lag = 3
        for n in range(N_CHUNKS + lag):
            if n < N_CHUNKS:
                take(it, order[n])
            if n >= lag:
                mix(it, order[n - lag])

    for it in range(2):
        for kind in range(4):
            for k in range(N_CHUNKS):
                remote(kind, it, k).wait_send()


def body(images, cotangent, *state):
    vmem = pl.BlockSpec(memory_space=pltpu.VMEM)
    hbm = pl.BlockSpec(memory_space=pl.ANY)
    pix = (SIDE, SIDE, CIN)
    pair = [pltpu.VMEM((2,) + s, BF16) for s in SHARDS]
    outs = pl.pallas_call(
        kernel,
        out_shape=[jax.ShapeDtypeStruct(s, F32) for s in SHARDS * 2],
        in_specs=[hbm] * 8,
        out_specs=[vmem] * 6,
        scratch_shapes=[
            pltpu.VMEM(pix, BF16), pltpu.VMEM(pix, BF16),
            pltpu.VMEM((ROWS, CIN), BF16), pltpu.VMEM((CIN, ROWS), BF16), pltpu.VMEM((ROWS, CIN), BF16),
            pltpu.VMEM((384, 384), BF16), pltpu.VMEM((384, 384), BF16),
            pltpu.VMEM((ROWS, 384), BF16), pltpu.VMEM((ROWS + 2 * PITCH, 384), BF16),
            pltpu.VMEM((MID, ROWS), BF16), pltpu.VMEM((ROWS, MID), BF16),
            pltpu.VMEM((ROWS, MID), F32), pltpu.VMEM((ROWS, MID), F32),
            pltpu.VMEM((ROWS, CIN), BF16),
        ]
        + [pltpu.VMEM(s, F32) for s in SHARDS] * 2
        + [pltpu.VMEM(s, F32) for s in FULLS]
        + [pltpu.VMEM((2,) + s, BF16) for s in FULLS]
        + pair * 6
        + [
            pltpu.SemaphoreType.DMA((4, 2, N_CHUNKS)),
            pltpu.SemaphoreType.DMA((4, 2, N_CHUNKS)),
            pltpu.SemaphoreType.DMA((8,)),
        ],
        compiler_params=pltpu.CompilerParams(
            collective_id=0, has_side_effects=True, vmem_limit_bytes=56 << 20
        ),
    )(images[0], cotangent[0], *[s[0] for s in state])
    return tuple(o[None] for o in outs)


def solution(mesh):
    pixels = P(("gossip", "dp"), None, None, None)
    rows, columns = P("gossip", "dp", None), P("gossip", None, "dp")
    return jax.shard_map(
        body,
        mesh=mesh,
        in_specs=(pixels, pixels) + (rows, rows, columns) * 2,
        out_specs=(rows, rows, columns) * 2,
        check_vma=False,
    )
```

time: 241 us -> 70.4 us (0.29)
  the two profiles are of different devices: /device:TPU:2 before, /device:TPU:56 now
where the time goes in v1:
time: 70.4 us; the launch traced here: 70.3 us
  Pallas kernels  63.3 us (90%)
  local copies, waits for them, and re-layouts  6.29 us (9%)
    pallas_call x1, Pallas kernels, body(): pl.pallas_call(kernel, out_shape=[jax.ShapeDtypeStruct(s, F32) for s in S...  63.3 us
    unnamed x14, local copies, waits for them, and re-layouts  6.29 us

profile of v1, /device:TPU:56, one launch (start us, length us, event | category | flops | bytes accessed | tf_op | source)
XLA Modules:
  0.0 70.3 jit_solution(15089642387303767597)
XLA Ops:
  0.6 63.3 %shard_map.127 = (f32[256,128]{1,0:T(8,128)}, f32[576,128]{1,0:T(8,128)}, f32[128,256]{1,0:T(8,128)}, f32[256,128]{1,0:T(8,128)}, f32[576,128]{1,0:T(8,128)}, /*index=5*/f32[128,256]{1,0:T(8,128)}) custom-call(bf16[28,28,512]{2,1,0:T(8,128)(2,1)} %bitcast.14, bf16[28,28,512]{2,1,0:T(8,128)(2,1)} %bitcast.15, f32[256,128]{1,0:T(8,128)} %bitcast.20, ...), custom_call_target="tpu_custom_call" | custom-call | tf_op jit(solution)/shard_map/pallas_call | solution.py:258
  64.0 1.6 %copy.20 = f32[1,256,128]{2,1,0:T(8,128)} copy(f32[1,256,128]{2,1,0:T(8,128)} %bitcast.27) | data formatting | bytes 262144
  65.5 0.0 copy-start.3
  65.5 0.0 copy-start.2
  65.5 1.7 %copy.21 = f32[1,576,128]{2,1,0:T(8,128)} copy(f32[1,576,128]{2,1,0:T(8,128)} %bitcast.19) | data formatting | bytes 589824
  67.3 0.0 copy-done.3
  67.3 0.0 copy-start
  67.3 0.7 copy.22
  67.9 0.0 copy-done.2
  67.9 0.7 copy.23
  68.6 0.0 copy-done
  68.6 0.0 copy-start.1
  68.6 0.7 %copy.24 = f32[1,576,128]{2,1,0:T(8,128)} copy(f32[1,576,128]{2,1,0:T(8,128)S(1)} %bitcast.18) | data formatting | bytes 589824
  69.3 0.3 copy-done.1
  69.6 0.7 copy.25
Async XLA Ops:
  65.5 1.7 %copy-start.3 = (f32[128,256]{1,0:T(8,128)S(1)}, f32[128,256]{1,0:T(8,128)}, u32[]{:S(2)}) copy-start(f32[128,256]{1,0:T(8,128)} %get-tuple-element.14) | copy-start | bytes 393220
  65.5 2.4 %copy-start.2 = (f32[256,128]{1,0:T(8,128)S(1)}, f32[256,128]{1,0:T(8,128)}, u32[]{:S(2)}) copy-start(f32[256,128]{1,0:T(8,128)} %get-tuple-element.15) | copy-start | bytes 393220
  67.3 1.3 %copy-start = (f32[576,128]{1,0:T(8,128)S(1)}, f32[576,128]{1,0:T(8,128)}, u32[]{:S(2)}) copy-start(f32[576,128]{1,0:T(8,128)} %get-tuple-element.16) | copy-start | bytes 884740
  68.6 1.0 %copy-start.1 = (f32[128,256]{1,0:T(8,128)S(1)}, f32[128,256]{1,0:T(8,128)}, u32[]{:S(2)}) copy-start(f32[128,256]{1,0:T(8,128)} %get-tuple-element.17) | copy-start | bytes 393220

commit v2 on v1

--- a/solution.py
+++ b/solution.py
@@ -24,6 +24,12 @@
 CHUNKS = ((0, 0, 256), (1, 0, 192), (1, 192, 192), (1, 384, 192), (2, 0, 128))
 N_CHUNKS = len(CHUNKS)
 E, W, G, M = range(4)
+ROUTES = {
+    (W, 0): {0: 1, 1: 1, 2: 2, 3: 2, 4: 0},
+    (W, 1): {0: 1, 1: 1, 2: 2, 3: 2, 4: 0},
+    (M, 0): {0: 1, 1: 2, 2: 2},
+    (M, 1): {4: 1, 1: 2, 2: 0},
+}
 
 
 def sigmoid(v):
@@ -59,7 +65,8 @@
         x_raw, c_raw, x, xt, cot, e2f, e2r, a1s, d2s, a1t, a2, slope1, slope2, d3,
         w1, w2, w3, m1, m2, m3, g1, g2, g3,
         e1, e2, e3, wb1, wb2, wb3, wa1, wa2, wa3, gb1, gb2, gb3, ga1, ga2, ga3,
-        mb1, mb2, mb3, ma1, ma2, ma3, send_sem, recv_sem, in_sem,
+        mb1, mb2, mb3, ma1, ma2, ma3,
+        rw1, rw2, rw3, rm1, rm2, rm3, send_sem, recv_sem, in_sem, relay_send, relay_recv,
     ) = refs[14:]
     w, m, g, e = (w1, w2, w3), (m1, m2, m3), (g1, g2, g3), (e1, e2, e3)
     wb, wa, gb, ga, mb, ma = (
@@ -73,11 +80,44 @@
         return (lax.rem(me + steps + count, count), dp)
 
     partner = (me, 1 - dp)
+    core, spot = lax.rem(me, 2), lax.rem(me, 64) // 2
+    x_lo = me // 64
+    far = 64 * (1 - x_lo)
+    last, origin = spot == 31, spot == 0
+    relays = (spot == 7) | (spot == 15) | (spot == 23)
+    relay_bufs = {W: (rw1, rw2, rw3), M: (rm1, rm2, rm3)}
 
     barrier = pltpu.get_barrier_semaphore()
     for other in (partner, at(1), at(-1), at(2), at(-2)):
         pl.semaphore_signal(barrier, inc=1, device_id=other, device_id_type=MESH)
 
+    def greet(other):
+        pl.semaphore_signal(barrier, inc=1, device_id=(other, dp), device_id_type=MESH)
+
+    @pl.when(last)
+    def _():
+        for y in range(3):
+            greet(64 * x_lo + 16 * y + 14 + core)
+
+    @pl.when(relays)
+    def _():
+        greet(64 * x_lo + 62 + core)
+        greet(far + core)
+
+        @pl.when(core == 1)
+        def _():
+            greet(far)
+
+    @pl.when(origin)
+    def _():
+        for y in range(3):
+            greet(far + 16 * y + 14 + core)
+
+            @pl.when(core == 0)
+            def _():
+                greet(far + 16 * y + 15)
+
+    guests = 5 + jnp.where(last, 3, 0) + jnp.where(relays, 2 + core, 0) + jnp.where(origin, 6 - 3 * core, 0)
     loads = {}
     for n, (src, dst) in enumerate(
         list(zip(w_in, w)) + [(images, x_raw), (cotangent, c_raw)] + list(zip(m_in, m))
@@ -102,6 +142,57 @@
             recv_sem=recv_sem.at[kind, it, k], device_id=to, device_id_type=MESH,
         )
 
+    def to_relay(kind, it, k):
+        idx, row, rows = CHUNKS[k]
+        rs = pl.ds(row, rows)
+        src = {W: wb, M: mb}[kind][idx].at[it, rs, :]
+        y = ROUTES[kind, it][k]
+        return pltpu.make_async_remote_copy(
+            src_ref=src, dst_ref=relay_bufs[kind][idx].at[it, rs, :],
+            send_sem=send_sem.at[kind, it, k], recv_sem=relay_recv.at[kind // 2, it, k],
+            device_id=(64 * x_lo + 16 * y + 14 + core, dp), device_id_type=MESH,
+        )
+
+    def from_relay(kind, it, k):
+        idx, row, rows = CHUNKS[k]
+        rs = pl.ds(row, rows)
+        return pltpu.make_async_remote_copy(
+            src_ref=relay_bufs[kind][idx].at[it, rs, :], dst_ref={W: wa, M: ma}[kind][idx].at[it, rs, :],
+            send_sem=relay_send.at[kind // 2, it, k], recv_sem=recv_sem.at[kind, it, k],
+            device_id=(far + it * core, dp), device_id_type=MESH,
+        )
+
+    def active(it, where):
+        return where if it == 1 else where & (core == 1)
+
+    def gossip(kind, it, k):
+        if k not in ROUTES[kind, it]:
+            remote(kind, it, k).start()
+            return
+        cross = active(it, last)
+
+        @pl.when(cross)
+        def _():
+            to_relay(kind, it, k).start()
+
+        @pl.when(jnp.logical_not(cross))
+        def _():
+            remote(kind, it, k).start()
+
+    def relay(kind, it, chunks, done=False):
+        for y in range(3):
+            mine = [k for k in chunks if ROUTES[kind, it].get(k) == y]
+            if mine:
+
+                @pl.when(active(it, spot == 8 * y + 7))
+                def _():
+                    for k in mine:
+                        if done:
+                            from_relay(kind, it, k).wait_send()
+                        else:
+                            to_relay(kind, it, k).wait_recv()
+                            from_relay(kind, it, k).start()
+
     def of(idx):
         return [k for k in range(N_CHUNKS) if CHUNKS[k][0] == idx]
 
@@ -110,9 +201,11 @@
         full = (0, SHARDS[idx][0])
         half(idx, e[idx].at[0], dp, *full)[...] = (w[idx][...] * SCALES[idx]).astype(BF16)
         wb[idx][0] = w[idx][...].astype(BF16)
-    pl.semaphore_wait(barrier, 5)
+    pl.semaphore_wait(barrier, guests)
     for k in range(N_CHUNKS):
         remote(E, 0, k).start()
+    for k in range(N_CHUNKS):
+        gossip(W, 0, k)
 
     d2s[...] = jnp.zeros_like(d2s)
     loads[3].wait()
@@ -133,7 +226,7 @@
         new = momentum_coef * m[idx][rs, :] + SCALES[idx] * total
         m[idx][rs, :] = new
         mb[idx][it, rs, :] = new.astype(BF16)
-        remote(M, it, k).start()
+        gossip(M, it, k)
 
     def mix(it, k):
         idx, row, rows = CHUNKS[k]
@@ -149,7 +242,7 @@
             half(idx, e[idx].at[1], dp, row, rows)[...] = (weight * SCALES[idx]).astype(BF16)
             remote(E, 1, k).start()
             wb[idx][1, rs, :] = weight.astype(BF16)
-            remote(W, 1, k).start()
+            gossip(W, 1, k)
         else:
             m_out[idx][rs, :] = mean
             w_out[idx][rs, :] = weight
@@ -190,9 +283,7 @@
         a2[...] = (h2 * sig).astype(BF16)
         for k in of(2):
             remote(E, it, k).wait_recv()
-        if it == 0:
-            for k in range(N_CHUNKS):
-                remote(W, 0, k).start()
+        relay(W, it, range(N_CHUNKS))
         for j in range(7):
             rs = pl.ds(j * 128, 128)
             pre = dot(a2[rs, :], e3[it]) + x[rs, :].astype(F32)
@@ -242,12 +333,23 @@
             if n < N_CHUNKS:
                 take(it, order[n])
             if n >= lag:
+                relay(M, it, (order[n - lag],))
                 mix(it, order[n - lag])
 
     for it in range(2):
         for kind in range(4):
             for k in range(N_CHUNKS):
                 remote(kind, it, k).wait_send()
+        for kind in (W, M):
+            relay(kind, it, range(N_CHUNKS), done=True)
+
+
+def write_out(*refs):
+    copies = [pltpu.make_async_copy(refs[i], refs[6 + i], refs[12].at[i]) for i in range(6)]
+    for c in copies:
+        c.start()
+    for c in copies:
+        c.wait()
 
 
 def body(images, cotangent, *state):
@@ -272,16 +374,25 @@
         + [pltpu.VMEM(s, F32) for s in SHARDS] * 2
         + [pltpu.VMEM(s, F32) for s in FULLS]
         + [pltpu.VMEM((2,) + s, BF16) for s in FULLS]
-        + pair * 6
+        + pair * 8
         + [
             pltpu.SemaphoreType.DMA((4, 2, N_CHUNKS)),
             pltpu.SemaphoreType.DMA((4, 2, N_CHUNKS)),
             pltpu.SemaphoreType.DMA((8,)),
+            pltpu.SemaphoreType.DMA((2, 2, N_CHUNKS)),
+            pltpu.SemaphoreType.DMA((2, 2, N_CHUNKS)),
         ],
         compiler_params=pltpu.CompilerParams(
             collective_id=0, has_side_effects=True, vmem_limit_bytes=56 << 20
         ),
     )(images[0], cotangent[0], *[s[0] for s in state])
+    outs = pl.pallas_call(
+        write_out,
+        out_shape=[jax.ShapeDtypeStruct(s, F32) for s in SHARDS * 2],
+        in_specs=[pl.BlockSpec(memory_space=pltpu.VMEM)] * 6,
+        out_specs=[pl.BlockSpec(memory_space=pltpu.HBM)] * 6,
+        scratch_shapes=[pltpu.SemaphoreType.DMA((6,))],
+    )(*outs)
     return tuple(o[None] for o in outs)
 
 

time: 70.4 us -> 57.8 us (0.82)
  the two profiles are of different devices: /device:TPU:56 before, /device:TPU:2 now
where the time goes in v2:
time: 57.8 us; the launch traced here: 57.2 us
  Pallas kernels  56.5 us (98%)
  between operations  0.64 us (1%)
    pallas_call x1, Pallas kernels, body(): pl.pallas_call(kernel, out_shape=[jax.ShapeDtypeStruct(s, F32) for s in S...  54.2 us
    pallas_call x1, Pallas kernels, body(): pl.pallas_call(write_out, out_shape=[jax.ShapeDtypeStruct(s, F32) for s i...  2.28 us

profile of v2, /device:TPU:2, one launch (start us, length us, event | category | flops | bytes accessed | tf_op | source)
XLA Modules:
  0.0 57.2 jit_solution(18254918744302326240)
XLA Ops:
  0.6 54.2 %shard_map.127 = (f32[256,128]{1,0:T(8,128)}, f32[576,128]{1,0:T(8,128)}, f32[128,256]{1,0:T(8,128)}, f32[256,128]{1,0:T(8,128)}, f32[576,128]{1,0:T(8,128)}, /*index=5*/f32[128,256]{1,0:T(8,128)}) custom-call(bf16[28,28,512]{2,1,0:T(8,128)(2,1)} %bitcast.14, bf16[28,28,512]{2,1,0:T(8,128)(2,1)} %bitcast.15, f32[256,128]{1,0:T(8,128)} %bitcast.18, ...), custom_call_target="tpu_custom_call" | custom-call | tf_op jit(solution)/shard_map/pallas_call | solution.py:360
  54.9 2.3 %shard_map.128 = (f32[256,128]{1,0:T(8,128)}, f32[576,128]{1,0:T(8,128)}, f32[128,256]{1,0:T(8,128)}, f32[256,128]{1,0:T(8,128)}, f32[576,128]{1,0:T(8,128)}, /*index=5*/f32[128,256]{1,0:T(8,128)}) custom-call(f32[256,128]{1,0:T(8,128)} %get-tuple-element.18.refs_0_, f32[576,128]{1,0:T(8,128)} %get-tuple-element.19.refs_1_, ...), custom_call_target="tpu_custom_call" | custom-call | tf_op jit(solution)/shard_map/pallas_call | solution.py:389

commit v3 on v2

--- a/solution.py
+++ b/solution.py
@@ -27,7 +27,7 @@
 ROUTES = {
     (W, 0): {0: 1, 1: 1, 2: 2, 3: 2, 4: 0},
     (W, 1): {0: 1, 1: 1, 2: 2, 3: 2, 4: 0},
-    (M, 0): {0: 1, 1: 2, 2: 2},
+    (M, 0): {3: 2, 4: 1},
     (M, 1): {4: 1, 1: 2, 2: 0},
 }
 
@@ -321,20 +321,20 @@
             middle()
             g3[...] = dot(a2[...].T, d3[...])
             send_grad(it, 2)
-            order = (0, 1, 2, 3, 4)
+            takes, mixes = (0, 1, 2, 3, 4), (0, 1, 2, 3, 4)
         else:
             middle()
             first()
             for k in range(N_CHUNKS):
                 remote(W, 1, k).wait_recv()
-            order = (4, 1, 2, 3, 0)
-        lag = 3
+            takes, mixes = (4, 1, 2, 3, 0), (4, 1, 2, 3, 0)
+        lag = 4
         for n in range(N_CHUNKS + lag):
             if n < N_CHUNKS:
-                take(it, order[n])
+                take(it, takes[n])
             if n >= lag:
-                relay(M, it, (order[n - lag],))
-                mix(it, order[n - lag])
+                relay(M, it, (mixes[n - lag],))
+                mix(it, mixes[n - lag])
 
     for it in range(2):
         for kind in range(4):

time: 57.8 us -> 54.6 us (0.945)
  Pallas kernels: 56.5 us -> 53.8 us
    pallas_call x1, Pallas kernels: 54.2 us -> 51.5 us  [body(): pl.pallas_call(kernel, out_shape=[jax.ShapeDtypeStruct(s, F32) for s in S...]
where the time goes in v3:
time: 54.6 us; the launch traced here: 54.4 us
  Pallas kernels  53.8 us (99%)
  between operations  0.64 us (1%)
    pallas_call x1, Pallas kernels, body(): pl.pallas_call(kernel, out_shape=[jax.ShapeDtypeStruct(s, F32) for s in S...  51.5 us
    pallas_call x1, Pallas kernels, body(): pl.pallas_call(write_out, out_shape=[jax.ShapeDtypeStruct(s, F32) for s i...  2.28 us

profile of v3, /device:TPU:2, one launch (start us, length us, event | category | flops | bytes accessed | tf_op | source)
XLA Modules:
  0.0 54.4 jit_solution(14215190186357011313)
XLA Ops:
  0.6 51.5 %shard_map.127 = (f32[256,128]{1,0:T(8,128)}, f32[576,128]{1,0:T(8,128)}, f32[128,256]{1,0:T(8,128)}, f32[256,128]{1,0:T(8,128)}, f32[576,128]{1,0:T(8,128)}, /*index=5*/f32[128,256]{1,0:T(8,128)}) custom-call(bf16[28,28,512]{2,1,0:T(8,128)(2,1)} %bitcast.14, bf16[28,28,512]{2,1,0:T(8,128)(2,1)} %bitcast.15, f32[256,128]{1,0:T(8,128)} %bitcast.18, ...), custom_call_target="tpu_custom_call" | custom-call | tf_op jit(solution)/shard_map/pallas_call | solution.py:360
  52.1 2.3 %shard_map.128 = (f32[256,128]{1,0:T(8,128)}, f32[576,128]{1,0:T(8,128)}, f32[128,256]{1,0:T(8,128)}, f32[256,128]{1,0:T(8,128)}, f32[576,128]{1,0:T(8,128)}, /*index=5*/f32[128,256]{1,0:T(8,128)}) custom-call(f32[256,128]{1,0:T(8,128)} %get-tuple-element.18.refs_0_, f32[576,128]{1,0:T(8,128)} %get-tuple-element.19.refs_1_, ...), custom_call_target="tpu_custom_call" | custom-call | tf_op jit(solution)/shard_map/pallas_call | solution.py:389

commit v4 on v3

--- a/solution.py
+++ b/solution.py
@@ -66,7 +66,7 @@
         w1, w2, w3, m1, m2, m3, g1, g2, g3,
         e1, e2, e3, wb1, wb2, wb3, wa1, wa2, wa3, gb1, gb2, gb3, ga1, ga2, ga3,
         mb1, mb2, mb3, ma1, ma2, ma3,
-        rw1, rw2, rw3, rm1, rm2, rm3, send_sem, recv_sem, in_sem, relay_send, relay_recv,
+        rw1, rw2, rw3, rm1, rm2, rm3, send_sem, recv_sem, in_sem, relay_send, relay_recv, out_sem,
     ) = refs[14:]
     w, m, g, e = (w1, w2, w3), (m1, m2, m3), (g1, g2, g3), (e1, e2, e3)
     wb, wa, gb, ga, mb, ma = (
@@ -193,6 +193,14 @@
                             to_relay(kind, it, k).wait_recv()
                             from_relay(kind, it, k).start()
 
+    def store(k):
+        idx, row, rows = CHUNKS[k]
+        rs = pl.ds(row, rows)
+        return (
+            pltpu.make_async_copy(w[idx].at[rs, :], w_out[idx].at[rs, :], out_sem.at[0, k]),
+            pltpu.make_async_copy(m[idx].at[rs, :], m_out[idx].at[rs, :], out_sem.at[1, k]),
+        )
+
     def of(idx):
         return [k for k in range(N_CHUNKS) if CHUNKS[k][0] == idx]
 
@@ -236,16 +244,16 @@
         if it == 0:
             remote(W, it, k).wait_recv()
         weight = 0.5 * (w[idx][rs, :] + wa[idx][it, rs, :].astype(F32)) - learn_rate * mean
+        m[idx][rs, :] = mean
+        w[idx][rs, :] = weight
         if it == 0:
-            m[idx][rs, :] = mean
-            w[idx][rs, :] = weight
             half(idx, e[idx].at[1], dp, row, rows)[...] = (weight * SCALES[idx]).astype(BF16)
             remote(E, 1, k).start()
             wb[idx][1, rs, :] = weight.astype(BF16)
             gossip(W, 1, k)
         else:
-            m_out[idx][rs, :] = mean
-            w_out[idx][rs, :] = weight
+            for copy in store(k):
+                copy.start()
 
     def send_grad(it, idx):
         for k in of(idx):
@@ -281,18 +289,24 @@
         sig = sigmoid(h2)
         slope2[...] = sig * (1.0 + h2 * (1.0 - sig))
         a2[...] = (h2 * sig).astype(BF16)
+        def out_half(which):
+            cols = pl.ds(pl.multiple_of(which * 256, 256), 256)
+            for j in range(7):
+                rs = pl.ds(j * 128, 128)
+                pre = dot(a2[rs, :], e3[it, :, cols]) + x[rs, cols].astype(F32)
+                sig = sigmoid(pre)
+                d3[rs, cols] = (cot[rs, cols].astype(F32) * (sig * (1.0 + pre * (1.0 - sig)))).astype(BF16)
+            return dot_nt(d3[:, cols], e3[it, :, cols])
+
+        da2 = out_half(dp)
         for k in of(2):
             remote(E, it, k).wait_recv()
         relay(W, it, range(N_CHUNKS))
-        for j in range(7):
-            rs = pl.ds(j * 128, 128)
-            pre = dot(a2[rs, :], e3[it]) + x[rs, :].astype(F32)
-            sig = sigmoid(pre)
-            d3[rs, :] = (cot[rs, :].astype(F32) * (sig * (1.0 + pre * (1.0 - sig)))).astype(BF16)
+        da2 = da2 + out_half(1 - dp)
         if it == 1:
             g3[...] = dot(a2[...].T, d3[...])
             send_grad(it, 2)
-        d2 = dot_nt(d3[...], e3[it]) * slope2[...]
+        d2 = da2 * slope2[...]
         inner = pl.ds(PITCH, ROWS)
         d2s[inner, 0:128] = pltpu.roll(d2, ROWS - 1, 0).astype(BF16)
         d2s[inner, 128:256] = d2.astype(BF16)
@@ -336,6 +350,9 @@
                 relay(M, it, (mixes[n - lag],))
                 mix(it, mixes[n - lag])
 
+    for k in range(N_CHUNKS):
+        for copy in store(k):
+            copy.wait()
     for it in range(2):
         for kind in range(4):
             for k in range(N_CHUNKS):
@@ -345,15 +362,19 @@
 
 
 def write_out(*refs):
-    copies = [pltpu.make_async_copy(refs[i], refs[6 + i], refs[12].at[i]) for i in range(6)]
-    for c in copies:
-        c.start()
-    for c in copies:
-        c.wait()
+    sem = refs[18]
+    loads = [pltpu.make_async_copy(refs[i], refs[12 + i], sem.at[0, i]) for i in range(6)]
+    stores = [pltpu.make_async_copy(refs[12 + i], refs[6 + i], sem.at[1, i]) for i in range(6)]
+    for copy in loads:
+        copy.start()
+    for load, copy in zip(loads, stores):
+        load.wait()
+        copy.start()
+    for copy in stores:
+        copy.wait()
 
 
 def body(images, cotangent, *state):
-    vmem = pl.BlockSpec(memory_space=pltpu.VMEM)
     hbm = pl.BlockSpec(memory_space=pl.ANY)
     pix = (SIDE, SIDE, CIN)
     pair = [pltpu.VMEM((2,) + s, BF16) for s in SHARDS]
@@ -361,7 +382,7 @@
         kernel,
         out_shape=[jax.ShapeDtypeStruct(s, F32) for s in SHARDS * 2],
         in_specs=[hbm] * 8,
-        out_specs=[vmem] * 6,
+        out_specs=[hbm] * 6,
         scratch_shapes=[
             pltpu.VMEM(pix, BF16), pltpu.VMEM(pix, BF16),
             pltpu.VMEM((ROWS, CIN), BF16), pltpu.VMEM((CIN, ROWS), BF16), pltpu.VMEM((ROWS, CIN), BF16),
@@ -381,6 +402,7 @@
             pltpu.SemaphoreType.DMA((8,)),
             pltpu.SemaphoreType.DMA((2, 2, N_CHUNKS)),
             pltpu.SemaphoreType.DMA((2, 2, N_CHUNKS)),
+            pltpu.SemaphoreType.DMA((2, N_CHUNKS)),
         ],
         compiler_params=pltpu.CompilerParams(
             collective_id=0, has_side_effects=True, vmem_limit_bytes=56 << 20
@@ -389,9 +411,10 @@
     outs = pl.pallas_call(
         write_out,
         out_shape=[jax.ShapeDtypeStruct(s, F32) for s in SHARDS * 2],
-        in_specs=[pl.BlockSpec(memory_space=pltpu.VMEM)] * 6,
-        out_specs=[pl.BlockSpec(memory_space=pltpu.HBM)] * 6,
-        scratch_shapes=[pltpu.SemaphoreType.DMA((6,))],
+        in_specs=[hbm] * 6,
+        out_specs=[hbm] * 6,
+        scratch_shapes=[pltpu.VMEM(s, F32) for s in SHARDS * 2] + [pltpu.SemaphoreType.DMA((2, 6))],
+        compiler_params=pltpu.CompilerParams(vmem_limit_bytes=60 << 20),
     )(*outs)
     return tuple(o[None] for o in outs)
 

time: 54.6 us -> 53.8 us (0.985)
  Pallas kernels: 53.8 us -> 53 us
    pallas_call x1, Pallas kernels: 51.5 us -> 50.9 us  [body(): pl.pallas_call(kernel, out_shape=[jax.ShapeDtypeStruct(s, F32) for s in S...]
where the time goes in v4:
time: 53.8 us; the launch traced here: 53.6 us
  Pallas kernels  53 us (99%)
  between operations  0.64 us (1%)
    pallas_call x1, Pallas kernels, body(): pl.pallas_call(kernel, out_shape=[jax.ShapeDtypeStruct(s, F32) for s in S...  50.9 us
    pallas_call x1, Pallas kernels, body(): pl.pallas_call(write_out, out_shape=[jax.ShapeDtypeStruct(s, F32) for s i...  2.08 us

profile of v4, /device:TPU:2, one launch (start us, length us, event | category | flops | bytes accessed | tf_op | source)
XLA Modules:
  0.0 53.6 jit_solution(17243030206402266138)
XLA Ops:
  0.6 50.9 %shard_map.127 = (f32[256,128]{1,0:T(8,128)}, f32[576,128]{1,0:T(8,128)}, f32[128,256]{1,0:T(8,128)}, f32[256,128]{1,0:T(8,128)}, f32[576,128]{1,0:T(8,128)}, /*index=5*/f32[128,256]{1,0:T(8,128)}) custom-call(bf16[28,28,512]{2,1,0:T(8,128)(2,1)} %bitcast.14, bf16[28,28,512]{2,1,0:T(8,128)(2,1)} %bitcast.15, f32[256,128]{1,0:T(8,128)} %bitcast.18, ...), custom_call_target="tpu_custom_call" | custom-call | tf_op jit(solution)/shard_map/pallas_call | solution.py:381
  51.5 2.1 %shard_map.128 = (f32[256,128]{1,0:T(8,128)}, f32[576,128]{1,0:T(8,128)}, f32[128,256]{1,0:T(8,128)}, f32[256,128]{1,0:T(8,128)}, f32[576,128]{1,0:T(8,128)}, /*index=5*/f32[128,256]{1,0:T(8,128)}) custom-call(f32[256,128]{1,0:T(8,128)} %get-tuple-element.18.refs_0_, f32[576,128]{1,0:T(8,128)} %get-tuple-element.19.refs_1_, ...), custom_call_target="tpu_custom_call" | custom-call | tf_op jit(solution)/shard_map/pallas_call | solution.py:411

commit v5 on v4

--- a/solution.py
+++ b/solution.py
@@ -262,9 +262,14 @@
             remote(G, it, k).start()
 
     for it in range(2):
+        def in_half(which):
+            chans = pl.ds(pl.multiple_of(which * 256, 256), 256)
+            return dot(x[:, chans], e1[it, chans, :])
+
+        h1 = in_half(dp)
         for k in of(0):
             remote(E, it, k).wait_recv()
-        h1 = dot(x[...], e1[it])
+        h1 = h1 + in_half(1 - dp)
         sig = sigmoid(h1)
         act1 = h1 * sig
         slope1[...] = sig * (1.0 + h1 * (1.0 - sig))

time: 53.8 us -> 53.8 us (level)
  no operation moved by 1% of the time
where the time goes in v5:
time: 53.8 us; the launch traced here: 53.6 us
  Pallas kernels  53 us (99%)
  between operations  0.64 us (1%)
    pallas_call x1, Pallas kernels, body(): pl.pallas_call(kernel, out_shape=[jax.ShapeDtypeStruct(s, F32) for s in S...  50.9 us
    pallas_call x1, Pallas kernels, body(): pl.pallas_call(write_out, out_shape=[jax.ShapeDtypeStruct(s, F32) for s i...  2.08 us

profile of v5, /device:TPU:2, one launch (start us, length us, event | category | flops | bytes accessed | tf_op | source)
XLA Modules:
  0.0 53.6 jit_solution(8420562712034218981)
XLA Ops:
  0.6 50.9 %shard_map.127 = (f32[256,128]{1,0:T(8,128)}, f32[576,128]{1,0:T(8,128)}, f32[128,256]{1,0:T(8,128)}, f32[256,128]{1,0:T(8,128)}, f32[576,128]{1,0:T(8,128)}, /*index=5*/f32[128,256]{1,0:T(8,128)}) custom-call(bf16[28,28,512]{2,1,0:T(8,128)(2,1)} %bitcast.14, bf16[28,28,512]{2,1,0:T(8,128)(2,1)} %bitcast.15, f32[256,128]{1,0:T(8,128)} %bitcast.18, ...), custom_call_target="tpu_custom_call" | custom-call | tf_op jit(solution)/shard_map/pallas_call | solution.py:386
  51.5 2.1 %shard_map.128 = (f32[256,128]{1,0:T(8,128)}, f32[576,128]{1,0:T(8,128)}, f32[128,256]{1,0:T(8,128)}, f32[256,128]{1,0:T(8,128)}, f32[576,128]{1,0:T(8,128)}, /*index=5*/f32[128,256]{1,0:T(8,128)}) custom-call(f32[256,128]{1,0:T(8,128)} %get-tuple-element.18.refs_0_, f32[576,128]{1,0:T(8,128)} %get-tuple-element.19.refs_1_, ...), custom_call_target="tpu_custom_call" | custom-call | tf_op jit(solution)/shard_map/pallas_call | solution.py:416
